TPU v7x, 32 devices: a whole 2x2x4 slice. The times are simulated.
32 devices in a mesh: groups: 4 (over y, x), shard: 8 (over z, core).
Axes of the slice: x: 2, y: 2, z: 4, core: 2. Of those that a mesh axis runs over, the one named last changes fastest.
Arguments:
- gradients: bfloat16 [4, 96, 1024, 1024], P('groups', None, 'shard'), may hold values from -200 to 200
- second_moment: bfloat16 [96, 1024, 1024], P('groups', 'shard'), may hold values from 0.25 to 4
- inverse_roots: bfloat16 [4, 8, 6, 2, 1024, 1024], P('groups', 'shard'), may hold values from -2 to 2
- owners: int32 [96], replicated, may hold values from 0 to 7, as said below
- weights: bfloat16 [96, 1024, 1024], P('groups', 'shard'), may hold values from -4 to 4
Outputs:
- new_weights: bfloat16 [96, 1024, 1024], P(None, 'shard')
Inputs may be any that keep to these rules, and one draw needn't show every extreme that they name: `owners`: blocks 24 * g to 24 * (g + 1) - 1 form group g. Within a group no owner is named by more than 6 blocks, and some owner is named by exactly 6.
All inputs are finite; a program needn't handle non-finite values.
Results may differ from a plain program's by a relative error of at most 0.0004.
The roundings to bfloat16 on the way count: a program that leaves them out, or rounds other values in their place, can miss the bound.
Values may be sent and summed in bfloat16 or wider, within the bound.
A program may use at most 256 MiB of HBM per device.

v0:
```python
import jax
import jax.numpy as jnp
from jax import lax
from jax.sharding import PartitionSpec as P


def body(gradients, second_moment, inverse_roots, owners, weights):
    groups_count = lax.axis_size("groups")
    shard_count = lax.axis_size("shard")
    group_index = lax.axis_index("groups")
    shard_index = lax.axis_index("shard")
    total_blocks = owners.shape[0]
    per_group = total_blocks // groups_count
    slot_count = inverse_roots.shape[2]
    row_count = gradients.shape[2]
    block_width = gradients.shape[3]
    group_start = group_index * per_group
    replica_grads = gradients[0].astype(jnp.float32)
    summed = lax.psum(replica_grads, "groups")
    group_grads = lax.dynamic_slice_in_dim(summed, group_start, per_group, 0)
    moment = 0.95 * second_moment.astype(jnp.float32) + 0.05 * group_grads * group_grads
    adam_step = group_grads / (jnp.sqrt(moment) + 1e-08)
    partial_sq = jnp.sum(adam_step * adam_step, axis=(1, 2))
    local_owner = lax.dynamic_slice_in_dim(owners, group_start, per_group, 0)
    same_owner = local_owner[:, None] == local_owner[None, :]
    block_ids = jnp.arange(per_group, dtype=jnp.int32)
    earlier = block_ids[None, :] < block_ids[:, None]
    position = jnp.sum(same_owner & earlier, axis=1)
    slot_ids = jnp.arange(slot_count, dtype=jnp.int32)
    dest_ids = jnp.arange(shard_count, dtype=jnp.int32)
    slot_match = (local_owner[None, None, :] == dest_ids[None, :, None]) & (
        position[None, None, :] == slot_ids[:, None, None]
    )
    present = jnp.any(slot_match, axis=2)
    source_block = jnp.sum(jnp.where(slot_match, block_ids[None, None, :], 0), axis=2)
    outgoing = jnp.take(group_grads, source_block.reshape(-1), axis=0).reshape(
        slot_count, shard_count, row_count, block_width
    )
    outgoing = jnp.where(present[:, :, None, None], outgoing, 0.0)
    graft_all = lax.psum(partial_sq, "shard")
    arrived = lax.all_to_all(outgoing, "shard", split_axis=1, concat_axis=2, tiled=True)
    mine_match = lax.dynamic_index_in_dim(slot_match, shard_index, 1, keepdims=False)
    graft_sq = jnp.sum(jnp.where(mine_match, graft_all[None, :], 0.0), axis=1)
    owned_blocks = arrived.reshape(slot_count, block_width, block_width)
    roots_mine = inverse_roots[0, 0]
    right_product = jnp.einsum(
        "mij,mjk->mik",
        owned_blocks,
        roots_mine[:, 1].astype(jnp.float32),
        precision=lax.Precision.HIGHEST,
    )
    preconditioned = jnp.einsum(
        "mij,mjk->mik",
        roots_mine[:, 0].astype(jnp.float32),
        right_product,
        precision=lax.Precision.HIGHEST,
    )
    graft_scale = jnp.sqrt(graft_sq) / jnp.sqrt(
        jnp.sum(preconditioned * preconditioned, axis=(1, 2)) + 1e-06
    )
    update = (graft_scale[:, None, None] * preconditioned).astype(jnp.bfloat16)
    update = update.reshape(slot_count, shard_count, row_count, block_width)
    returned = lax.all_to_all(update, "shard", split_axis=1, concat_axis=1, tiled=True)
    returned_flat = returned.reshape(slot_count * shard_count, row_count, block_width)
    mine_update = jnp.take(returned_flat, position * shard_count + local_owner, axis=0)
    own_weights = weights.astype(jnp.float32)
    stepped = own_weights - 0.5 * mine_update.astype(jnp.float32)
    renormed = (
        stepped * lax.rsqrt(jnp.mean(stepped * stepped, axis=2, keepdims=True) + 1e-06)
    ).astype(jnp.bfloat16)
    return lax.all_gather(renormed, "groups", axis=0, tiled=True)


def solution(mesh):
    return jax.shard_map(
        body,
        mesh=mesh,
        in_specs=(
            P("groups", None, "shard", None),
            P("groups", "shard", None),
            P("groups", "shard", None, None, None, None),
            P(),
            P("groups", "shard", None),
        ),
        out_specs=P(None, "shard", None),
        check_vma=False,
    )
```

profile of v0, /device:TPU:0, one launch (start us, length us, event | category | flops | bytes accessed | tf_op | source)
XLA Modules:
  0.0 2195.3 jit_solution(18141801697823471418)
XLA Ops:
  6.5 0.0 all-reduce.2.cloned.1.call-start
  6.5 27.3 %bitcast_convert_fusion = f32[96,128,1024]{2,1,0:T(8,128)} fusion(bf16[1,96,128,1024]{3,2,1,0:T(8,128)(2,1)} %param.5), kind=kLoop, calls=%fused_computation.2 | loop fusion | flops 12582912 | bytes 75497472 | tf_op jit(solution)/shard_map/convert_element_type | solution.py:18
  33.8 0.0 copy-start.1
  33.8 0.0 all-reduce.2.cloned.1.call-update
  33.8 0.6 copy-done.1
  34.5 0.1 dynamic_slice.10
  34.5 0.2 convert_reduce_fusion
  34.7 0.0 copy-start.3
  34.7 0.6 copy-done.3
  35.3 0.2 select_reduce_fusion
  35.5 0.1 copy.23
  35.6 0.1 reshape.126
  35.7 0.1 copy.22
  35.8 0.2 broadcast_and_fusion
  36.0 0.1 copy.21
  36.1 851.7 %all-reduce.2.cloned.1.call-done = f32[96,128,1024]{2,1,0:T(8,128)} async-done(((f32[96,128,1024]{2,1,0:T(8,128)}), f32[96,128,1024]{2,1,0:T(8,128)}) %all-reduce.2.cloned.1.call-update) | async-done | bytes 50331664 | tf_op jit(solution)/shard_map/psum | solution.py:19
  887.8 15.9 fusion.7
  903.7 15.8 gather_fusion
  919.5 10.2 select_select_fusion
  929.7 8.8 copy.24
  938.4 6.4 all-to-all-start
  944.9 20.6 copy.30
  965.5 396.5 %psum.15 = f32[24]{0:T(128)S(1)} all-reduce(f32[24]{0:T(128)S(1)} %get-tuple-element.7), channel_id=1, replica_groups=mesh['groups'=4,'shard'=8] {'shard'}, use_global_device_ids=true, to_apply=%region_3.0 | all-reduce | flops 24 | bytes 192 | tf_op jit(solution)/shard_map/psum | solution.py:40
  1362.0 0.1 select_reduce_fusion.1
  1362.2 126.3 %all-to-all-done = f32[6,8,128,1024]{3,2,0,1:T(8,128)} async-done(((f32[6,8,128,1024]{3,2,0,1:T(8,128)}), f32[6,8,128,1024]{3,2,0,1:T(8,128)}, u32[]{:S(2)}, u32[]{:S(2)}) %all-to-all-start) | async-done | bytes 25165856 | tf_op jit(solution)/shard_map/all_to_all | solution.py:41
  1488.5 0.0 copy-start
  1488.5 18.9 copy.25
  1507.4 5.2 copy-done
  1512.6 44.4 %fusion.6 = f32[6,1024,1024]{2,1,0:T(8,128)} fusion(f32[6,1024,1024]{2,1,0:T(8,128)} %bitcast.33, bf16[6,2,1024,1024]{3,2,0,1:T(8,128)(2,1)S(1)} %bitcast.31), kind=kOutput, calls=%fused_computation.16 | convolution fusion | flops 77309411328 | bytes 62914560 | tf_op jit(solution)/shard_map/mij,mjk->mik/dot_general | solution.py:46
  1557.0 48.6 %multiply_reduce_fusion = (f32[6]{0:T(128)S(1)}, f32[6,1024,1024]{1,2,0:T(8,128)}) fusion(f32[6,1024,1024]{2,1,0:T(8,128)} %fusion.6, bf16[6,2,1024,1024]{3,2,0,1:T(8,128)(2,1)S(1)} %bitcast.32), kind=kOutput, calls=%fused_computation.5 | convolution fusion | flops 77321994240 | bytes 62914584 | tf_op jit(solution)/shard_map/mij,mjk->mik/dot_general | solution.py:52
  1605.6 10.3 multiply_convert_fusion
  1615.9 5.8 copy.27
  1621.7 0.0 copy-start.2
  1621.7 8.6 all-to-all-start.1
  1630.3 0.0 all-gather.2.cloned.1.call-start
  1630.3 0.0 copy-done.2
  1630.3 0.0 copy-done.4
  1630.4 0.1 compare_and_fusion.1
  1630.5 273.7 %all-to-all-done.1 = bf16[6,8,128,1024]{3,2,0,1:T(8,128)(2,1)} async-done(((bf16[6,8,128,1024]{3,2,0,1:T(8,128)(2,1)}), bf16[6,8,128,1024]{3,2,0,1:T(8,128)(2,1)}, u32[]{:S(2)}, u32[]{:S(2)}) %all-to-all-start.1) | async-done | bytes 12582944 | tf_op jit(solution)/shard_map/all_to_all | solution.py:63
  1904.2 10.5 copy.28
  1914.7 9.0 gather_fusion.1
  1923.7 7.7 multiply_reduce_fusion.1
  1931.5 0.0 slice-done
  1931.5 0.0 slice-done.1
  1931.5 8.0 multiply_convert_fusion.1
  1939.5 0.0 all-gather.2.cloned.1.call-update
  1939.5 228.3 %all-gather.2.cloned.1.call-done = bf16[96,128,1024]{2,1,0:T(8,128)(2,1)} async-done(((bf16[24,128,1024]{2,1,0:T(8,128)(2,1)}), bf16[96,128,1024]{2,1,0:T(8,128)(2,1)}) %all-gather.2.cloned.1.call-update) | async-done | bytes 25165840 | tf_op jit(solution)/shard_map/all_gather | solution.py:71
  2167.8 20.6 copy.33
  (12 shorter events, 0.1 us)
Async XLA Ops:
  6.5 881.3 %all-reduce.2.cloned.1.call-start = ((), (), s32[]{:S(2)}) async-start(), calls=%async_computation.2 | async-start | bytes 100663296 | tf_op jit(solution)/shard_map/psum | solution.py:19
  33.8 0.7 copy-start.1
  34.7 0.6 copy-start.3
  938.4 550.0 %all-to-all-start = ((f32[6,8,128,1024]{3,2,0,1:T(8,128)}), f32[6,8,128,1024]{3,2,0,1:T(8,128)}, u32[]{:S(2)}, u32[]{:S(2)}) async-start(f32[6,8,128,1024]{3,2,0,1:T(8,128)} %copy.24), calls=%async_computation | async-start | bytes 50331648 | tf_op jit(solution)/shard_map/all_to_all | solution.py:41
  1488.5 24.1 %copy-start = (bf16[1,1,6,2,1024,1024]{5,4,2,3,1,0:T(8,128)(2,1)S(1)}, bf16[1,1,6,2,1024,1024]{5,4,2,3,1,0:T(8,128)(2,1)}, u32[]{:S(2)}) copy-start(bf16[1,1,6,2,1024,1024]{5,4,2,3,1,0:T(8,128)(2,1)} %copy.30) | copy-start | bytes 75497472
  1621.7 8.6 copy-start.2
  1621.7 8.6 copy-start.4
  1621.7 282.5 %all-to-all-start.1 = ((bf16[6,8,128,1024]{3,2,0,1:T(8,128)(2,1)}), bf16[6,8,128,1024]{3,2,0,1:T(8,128)(2,1)}, u32[]{:S(2)}, u32[]{:S(2)}) async-start(bf16[6,8,128,1024]{3,2,0,1:T(8,128)(2,1)} %copy.27), calls=%async_computation.1 | async-start | bytes 25165824 | tf_op jit(solution)/shard_map/all_to_all | solution.py:63
  1630.3 537.5 %all-gather.2.cloned.1.call-start = ((), (), s32[]{:S(2)}) async-start(), calls=%async_computation.3 | async-start | bytes 31457280 | tf_op jit(solution)/shard_map/all_gather | solution.py:71
  1923.7 7.8 slice-start
  1923.7 7.8 slice-start.1
Sparse Core Ops, SparseCore 0:
  33.9 853.8 all-reduce.1
  1939.6 228.0 all-gather.1
where the time goes:
time: 2200 us
  waiting for transfers between devices  1480 us (67%)
  blocking collectives  397 us (18%)
  local copies, waits for them, and re-layouts  117 us (5%)
  matrix products  93 us (4%)
  other arithmetic  80.2 us (4%)
    psum x1, waiting for transfers between devices, body(): summed = lax.psum(replica_grads, 'groups')  852 us
    psum x1, blocking collectives, body(): graft_all = lax.psum(partial_sq, 'shard')  397 us
    all_to_all x1, waiting for transfers between devices, body(): lax.all_to_all(update, 'shard', split_axis=1, concat_axis=1, tiled=True)  274 us
    all_gather x1, waiting for transfers between devices, body(): return lax.all_gather(renormed, 'groups', axis=0, tiled=True)  228 us
    all_to_all x1, waiting for transfers between devices, body(): lax.all_to_all(outgoing, 'shard', split_axis=1, concat_axis=2, tiled=True)  126 us
    dot_general x1, matrix products, body(): jnp.einsum('mij,mjk->mik', roots_mine[:, 0].astype(jnp.float32), right_pr...  48.6 us
    unnamed x16, local copies, waits for them, and re-layouts  47.7 us
    dot_general x1, matrix products, body(): jnp.einsum('mij,mjk->mik', owned_blocks, roots_mine[:, 1].astype(jnp.floa...  44.4 us
  transfers between devices with their start and end apart: 4, of which 4 were waited for; matrix products, arithmetic and copies ran while one was open for 1% of the time, Pallas kernels for 0%

commit v1 on v0

v1 whole, which is shorter than its diff:
```python
import jax
import jax.numpy as jnp
from jax import lax
from jax.experimental import pallas as pl
from jax.experimental.pallas import tpu as pltpu
from jax.sharding import PartitionSpec as P


def split(value):
    high = lax.reduce_precision(value, 8, 7)
    low = value - high
    return high.astype(jnp.bfloat16), low.astype(jnp.bfloat16)


def product(left, right):
    return jnp.einsum(
        "mij,mjk->mik", left, right, preferred_element_type=jnp.float32
    )


def pack_kernel(order, present, replicas, moments, packed, squares):
    slot = pl.program_id(0)
    total = replicas[0, 0].astype(jnp.float32)
    for replica in range(1, replicas.shape[0]):
        total = total + replicas[replica, 0].astype(jnp.float32)
    total = jnp.where(present[slot] > 0, total, 0.0)
    high = total.astype(jnp.bfloat16)
    packed[0, 0] = high
    packed[1, 0] = (total - high.astype(jnp.float32)).astype(jnp.bfloat16)
    moment = 0.95 * moments[0].astype(jnp.float32) + 0.05 * total * total
    adam_step = total / (jnp.sqrt(moment) + 1e-08)
    square = adam_step * adam_step
    rows, width = square.shape
    squares[0] = jnp.sum(square.reshape(rows // 8, 8, width), axis=0)


def pack(order, present, replicas, moments):
    groups, _, rows, width = replicas.shape
    slots = order.shape[0]
    return pl.pallas_call(
        pack_kernel,
        grid_spec=pltpu.PrefetchScalarGridSpec(
            num_scalar_prefetch=2,
            grid=(slots,),
            in_specs=[
                pl.BlockSpec((groups, 1, rows, width), lambda s, o, p: (0, o[s], 0, 0)),
                pl.BlockSpec((1, rows, width), lambda s, o, p: (o[s], 0, 0)),
            ],
            out_specs=[
                pl.BlockSpec((2, 1, rows, width), lambda s, o, p: (0, s, 0, 0)),
                pl.BlockSpec((1, 8, width), lambda s, o, p: (s, 0, 0)),
            ],
        ),
        out_shape=[
            jax.ShapeDtypeStruct((2, slots, rows, width), jnp.bfloat16),
            jax.ShapeDtypeStruct((slots, 8, width), jnp.float32),
        ],
        compiler_params=pltpu.CompilerParams(vmem_limit_bytes=24 * 1024 * 1024),
    )(order, present, replicas, moments)


def step_kernel(place, returned, weights, renormed):
    stepped = weights[0].astype(jnp.float32) - 0.5 * returned[0].astype(jnp.float32)
    mean = jnp.mean(stepped * stepped, axis=1, keepdims=True)
    renormed[0] = (stepped * lax.rsqrt(mean + 1e-06)).astype(jnp.bfloat16)


def step(place, returned, weights):
    blocks, rows, width = weights.shape
    return pl.pallas_call(
        step_kernel,
        grid_spec=pltpu.PrefetchScalarGridSpec(
            num_scalar_prefetch=1,
            grid=(blocks,),
            in_specs=[
                pl.BlockSpec((1, rows, width), lambda b, p: (p[b], 0, 0)),
                pl.BlockSpec((1, rows, width), lambda b, p: (b, 0, 0)),
            ],
            out_specs=pl.BlockSpec((1, rows, width), lambda b, p: (b, 0, 0)),
        ),
        out_shape=jax.ShapeDtypeStruct(weights.shape, jnp.bfloat16),
        compiler_params=pltpu.CompilerParams(vmem_limit_bytes=24 * 1024 * 1024),
    )(place, returned, weights)


def body(gradients, second_moment, inverse_roots, owners, weights):
    groups_count = lax.axis_size("groups")
    shard_count = lax.axis_size("shard")
    group_index = lax.axis_index("groups")
    shard_index = lax.axis_index("shard")
    total_blocks = owners.shape[0]
    per_group = total_blocks // groups_count
    slot_count = inverse_roots.shape[2]
    row_count = gradients.shape[2]
    block_width = gradients.shape[3]
    group_start = group_index * per_group

    local_owner = lax.dynamic_slice_in_dim(owners, group_start, per_group, 0)
    same_owner = local_owner[:, None] == local_owner[None, :]
    block_ids = jnp.arange(per_group, dtype=jnp.int32)
    earlier = block_ids[None, :] < block_ids[:, None]
    position = jnp.sum(same_owner & earlier, axis=1).astype(jnp.int32)
    slot_ids = jnp.arange(slot_count, dtype=jnp.int32)
    dest_ids = jnp.arange(shard_count, dtype=jnp.int32)
    slot_match = (local_owner[None, None, :] == dest_ids[None, :, None]) & (
        position[None, None, :] == slot_ids[:, None, None]
    )
    present = jnp.any(slot_match, axis=2).astype(jnp.int32).reshape(-1)
    order = jnp.sum(jnp.where(slot_match, block_ids[None, None, :], 0), axis=2)
    order = order.astype(jnp.int32).reshape(-1)

    replicas = lax.all_to_all(
        gradients.reshape(groups_count, per_group, row_count, block_width),
        "groups",
        split_axis=0,
        concat_axis=0,
        tiled=True,
    )
    packed, squares = pack(order, present, replicas, second_moment)
    graft_all = lax.psum(jnp.sum(squares, axis=(1, 2)), "shard")
    graft_sq = lax.dynamic_index_in_dim(
        graft_all.reshape(slot_count, shard_count), shard_index, 1, keepdims=False
    )
    outgoing = packed.reshape(2, slot_count, shard_count, row_count, block_width)
    arrived = lax.all_to_all(outgoing, "shard", split_axis=2, concat_axis=2, tiled=True)
    arrived = arrived.reshape(2, slot_count, block_width, block_width)
    roots_mine = inverse_roots[0, 0]
    left, right = roots_mine[:, 0], roots_mine[:, 1]
    right_product = product(arrived[0], right) + product(arrived[1], right)
    high, low = split(right_product)
    preconditioned = product(left, high) + product(left, low)
    graft_scale = jnp.sqrt(graft_sq) / jnp.sqrt(
        jnp.sum(preconditioned * preconditioned, axis=(1, 2)) + 1e-06
    )
    update = (graft_scale[:, None, None] * preconditioned).astype(jnp.bfloat16)
    update = update.reshape(slot_count, shard_count, row_count, block_width)
    returned = lax.all_to_all(update, "shard", split_axis=1, concat_axis=1, tiled=True)
    returned = returned.reshape(slot_count * shard_count, row_count, block_width)
    renormed = step(position * shard_count + local_owner, returned, weights)
    return lax.all_gather(renormed, "groups", axis=0, tiled=True)


def solution(mesh):
    return jax.shard_map(
        body,
        mesh=mesh,
        in_specs=(
            P("groups", None, "shard", None),
            P("groups", "shard", None),
            P("groups", "shard", None, None, None, None),
            P(),
            P("groups", "shard", None),
        ),
        out_specs=P(None, "shard", None),
        check_vma=False,
    )
```

time: 2200 us -> 1610 us (0.73)
  waiting for transfers between devices: 1480 us -> 899 us
  other arithmetic: 80.2 us -> 11.4 us
  Pallas kernels: 0 us -> 48.9 us
    psum x1 -> x0, waiting for transfers between devices: 852 us -> none  [body(): summed = lax.psum(replica_grads, 'groups')]
    all_to_all x1 -> x2, waiting for transfers between devices: 126 us -> 398 us  [the longest x1 272 us: body(): lax.all_to_all(gradients.reshape(groups_count, per_group, row_count, bloc...]
    pallas_call x0 -> x2, Pallas kernels: none -> 48.9 us  [the longest x1 43.6 us: pack(): pl.pallas_call(pack_kernel, grid_spec=pltpu.PrefetchScalarGridSpec(num_sc...]
    convert_element_type x2 -> x1, other arithmetic: 35.2 us -> 0.01 us  [body(): present = jnp.any(slot_match, axis=2).astype(jnp.int32).reshape(-1)]
    gather x2 -> x0, local copies, waits for them, and re-layouts: 24.8 us -> none  [the longest x1 15.8 us: body(): jnp.take(group_grads, source_block.reshape(-1), axis=0)]
    reduce_sum x5 -> x3, other arithmetic: 24.1 us -> 0.8 us  [the longest x1 0.44 us: body(): graft_all = lax.psum(jnp.sum(squares, axis=(1, 2)), 'shard')]
    dot_general x2 -> x4, matrix products: 93 us -> 114 us  [product(): jnp.einsum('mij,mjk->mik', left, right, preferred_element_type=jnp.float32)]
where the time goes in v1:
time: 1610 us
  waiting for transfers between devices  899 us (56%)
  blocking collectives  396 us (25%)
  matrix products  114 us (7%)
  local copies, waits for them, and re-layouts  104 us (6%)
  Pallas kernels  48.9 us (3%)
  starting transfers between devices  23.8 us (1%)
    psum x1, blocking collectives, body(): graft_all = lax.psum(jnp.sum(squares, axis=(1, 2)), 'shard')  396 us
    all_to_all x1, waiting for transfers between devices, body(): lax.all_to_all(update, 'shard', split_axis=1, concat_axis=1, tiled=True)  274 us
    all_to_all x1, waiting for transfers between devices, body(): lax.all_to_all(gradients.reshape(groups_count, per_group, row_count, bloc...  272 us
    all_gather x1, waiting for transfers between devices, body(): return lax.all_gather(renormed, 'groups', axis=0, tiled=True)  227 us
    all_to_all x1, waiting for transfers between devices, body(): lax.all_to_all(outgoing, 'shard', split_axis=2, concat_axis=2, tiled=True)  126 us
    dot_general x4, matrix products, product(): jnp.einsum('mij,mjk->mik', left, right, preferred_element_type=jnp.float32)  114 us
    unnamed x16, local copies, waits for them, and re-layouts  50.1 us
    pallas_call x1, Pallas kernels, pack(): pl.pallas_call(pack_kernel, grid_spec=pltpu.PrefetchScalarGridSpec(num_sc...  43.6 us
  transfers between devices with their start and end apart: 4, of which 4 were waited for; matrix products, arithmetic and copies ran while one was open for 1% of the time, Pallas kernels for 0%

profile of v1, /device:TPU:0, one launch (start us, length us, event | category | flops | bytes accessed | tf_op | source)
XLA Modules:
  0.0 1610.4 jit_solution(1450679252134518340)
XLA Ops:
  6.5 0.0 copy-start.3
  6.5 8.6 all-to-all-start
  15.1 0.0 copy-done.3
  15.1 0.1 dynamic_slice.7
  15.2 0.2 convert_reduce_fusion
  15.4 0.0 copy-start.5
  15.4 0.5 copy-done.5
  15.9 0.2 fusion.9
  16.1 0.1 reshape.86.order
  16.2 0.2 and_reduce_fusion
  16.4 0.1 reshape.92.present
  16.5 272.2 %all-to-all-done.replicas = bf16[4,24,128,1024]{3,2,1,0:T(8,128)(2,1)} async-done(((bf16[4,24,128,1024]{3,2,1,0:T(8,128)(2,1)}), bf16[4,24,128,1024]{3,2,1,0:T(8,128)(2,1)}, u32[]{:S(2)}, u32[]{:S(2)}) %all-to-all-start) | async-done | bytes 25165856 | tf_op jit(solution)/shard_map/all_to_all | solution.py:112
  288.7 2.8 copy-done.1
  291.5 43.6 %shard_map.55 = (bf16[2,48,128,1024]{3,2,1,0:T(8,128)(2,1)}, f32[48,8,1024]{2,1,0:T(8,128)S(1)}) custom-call(s32[48]{0:T(128)S(1)} %reshape.86.order, s32[48]{0:T(128)S(1)} %reshape.92.present, bf16[4,24,128,1024]{3,2,1,0:T(8,128)(2,1)} %all-to-all-done.replicas, bf16[24,128,1024]{2,1,0:T(8,128)(2,1)S(1)} %copy-done.1), custom_call_target="tpu_custom_call" | custom-call | tf_op jit(solution)/shard_map/pallas_call | solution.py:40
  335.1 20.6 %copy.14 = bf16[2,6,8,128,1024]{4,3,1,0,2:T(8,128)(2,1)} copy(bf16[2,6,8,128,1024]{4,3,2,1,0:T(8,128)(2,1)} %bitcast.32) | data formatting | bytes 50331648 | tf_op jit(solution)/shard_map/reshape | solution.py:124
  355.7 6.4 all-to-all-start.1
  362.1 20.7 %copy.21 = bf16[1,1,6,2,1024,1024]{5,4,2,3,1,0:T(8,128)(2,1)} copy(bf16[1,1,6,2,1024,1024]{5,4,3,2,1,0:T(8,128)(2,1)} %param.7) | data formatting | bytes 50331648 | tf_op args[2]
  382.8 0.4 reduce_sum.38
  383.2 0.1 reshape.88
  383.3 396.1 %psum.7 = f32[6,8]{1,0:T(8,128)S(1)} all-reduce(f32[6,8]{1,0:T(8,128)S(1)} %reshape.88), channel_id=1, replica_groups=mesh['groups'=4,'shard'=8] {'shard'}, use_global_device_ids=true, to_apply=%region_4.5 | all-reduce | flops 48 | bytes 384 | tf_op jit(solution)/shard_map/psum | solution.py:120
  779.4 0.2 sqrt_reduce_fusion
  779.6 126.1 %all-to-all-done.1 = bf16[2,6,8,128,1024]{4,3,1,0,2:T(8,128)(2,1)} async-done(((bf16[2,6,8,128,1024]{4,3,1,0,2:T(8,128)(2,1)}), bf16[2,6,8,128,1024]{4,3,1,0,2:T(8,128)(2,1)}, u32[]{:S(2)}, u32[]{:S(2)}) %all-to-all-start.1) | async-done | bytes 25165856 | tf_op jit(solution)/shard_map/all_to_all | solution.py:125
  905.7 9.9 fusion.11
  915.6 5.3 copy.17
  921.0 5.2 copy.15
  926.1 23.3 %fusion.4 = f32[6,1024,1024]{2,1,0:T(8,128)} fusion(bf16[6,1024,1024]{2,1,0:T(8,128)(2,1)} %bitcast.33, bf16[6,2,1024,1024]{3,2,0,1:T(8,128)(2,1)} %bitcast.26), kind=kOutput, calls=%fused_computation.10 | convolution fusion | flops 12884901888 | bytes 50331648 | tf_op jit(solution)/shard_map/mij,mjk->mik/dot_general | solution.py:16
  949.4 23.3 %fusion.5 = f32[6,1024,1024]{2,1,0:T(8,128)} fusion(bf16[6,1024,1024]{2,1,0:T(8,128)(2,1)} %bitcast.34, bf16[6,2,1024,1024]{3,2,0,1:T(8,128)(2,1)} %bitcast.27), kind=kOutput, calls=%fused_computation.11 | convolution fusion | flops 12884901888 | bytes 50331648 | tf_op jit(solution)/shard_map/mij,mjk->mik/dot_general | solution.py:16
  972.8 30.6 %fusion.1 = f32[6,1024,1024]{1,2,0:T(8,128)} fusion(bf16[6,2,1024,1024]{3,2,0,1:T(8,128)(2,1)} %bitcast.28, f32[6,1024,1024]{2,1,0:T(8,128)} %fusion.5, f32[6,1024,1024]{2,1,0:T(8,128)} %fusion.4), kind=kOutput, calls=%fused_computation.6 | convolution fusion | flops 12910067712 | bytes 88080384 | tf_op jit(solution)/shard_map/mij,mjk->mik/dot_general | solution.py:16
  1003.3 36.9 %multiply_reduce_fusion = (f32[6]{0:T(128)S(1)}, f32[6,1024,1024]{1,2,0:T(8,128)}) fusion(f32[6,1024,1024]{1,2,0:T(8,128)} %fusion.1, f32[6,1024,1024]{2,1,0:T(8,128)} %fusion.5, f32[6,1024,1024]{2,1,0:T(8,128)} %fusion.4, bf16[6,2,1024,1024]{3,2,0,1:T(8,128)(2,1)} %bitcast.29), kind=kOutput, calls=%fused_computation.5 | convolution fusion | flops 12922650624 | bytes 113246232 | tf_op jit(solution)/shard_map/mij,mjk->mik/dot_general | solution.py:16
  1040.3 10.3 multiply_convert_fusion
  1050.6 0.0 copy-start.4
  1050.6 0.0 copy-start.6
  1050.6 5.8 copy.18
  1056.4 8.7 all-to-all-start.2
  1065.1 0.0 all-gather.2.cloned.1.call-start
  1065.1 0.0 copy-done.4
  1065.2 0.0 copy-done.6
  1065.2 0.1 multiply_add_fusion.place
  1065.2 273.7 %all-to-all-done.2 = bf16[6,8,128,1024]{3,2,0,1:T(8,128)(2,1)} async-done(((bf16[6,8,128,1024]{3,2,0,1:T(8,128)(2,1)}), bf16[6,8,128,1024]{3,2,0,1:T(8,128)(2,1)}, u32[]{:S(2)}, u32[]{:S(2)}) %all-to-all-start.2) | async-done | bytes 12582944 | tf_op jit(solution)/shard_map/all_to_all | solution.py:137
  1339.0 6.3 copy.19
  1345.3 0.0 copy-start.2
  1345.3 2.8 copy-done.2
  1348.1 5.2 shard_map.56
  1353.3 0.0 copy-start
  1353.3 2.7 copy-done
  1356.0 0.0 all-gather.2.cloned.1.call-update
  1356.1 226.8 %all-gather.2.cloned.1.call-done = bf16[96,128,1024]{2,1,0:T(8,128)(2,1)} async-done(((bf16[24,128,1024]{2,1,0:T(8,128)(2,1)}), bf16[96,128,1024]{2,1,0:T(8,128)(2,1)}) %all-gather.2.cloned.1.call-update) | async-done | bytes 25165840 | tf_op jit(solution)/shard_map/all_gather | solution.py:140
  1582.9 20.6 %copy.23 = bf16[96,128,1024]{2,1,0:T(8,128)(2,1)} copy(bf16[96,128,1024]{2,1,0:T(8,128)(2,1)} %all-gather.2.cloned.1.call-done) | data formatting | bytes 50331648
  (5 shorter events, 0.0 us)
Async XLA Ops:
  6.5 8.6 copy-start.3
  6.5 282.1 %all-to-all-start = ((bf16[4,24,128,1024]{3,2,1,0:T(8,128)(2,1)}), bf16[4,24,128,1024]{3,2,1,0:T(8,128)(2,1)}, u32[]{:S(2)}, u32[]{:S(2)}) async-start(bf16[4,24,128,1024]{3,2,1,0:T(8,128)(2,1)} %bitcast.31), calls=%async_computation | async-start | bytes 50331648 | tf_op jit(solution)/shard_map/all_to_all | solution.py:112
  15.4 0.6 copy-start.5
  288.7 2.8 copy-start.1
  355.7 550.0 %all-to-all-start.1 = ((bf16[2,6,8,128,1024]{4,3,1,0,2:T(8,128)(2,1)}), bf16[2,6,8,128,1024]{4,3,1,0,2:T(8,128)(2,1)}, u32[]{:S(2)}, u32[]{:S(2)}) async-start(bf16[2,6,8,128,1024]{4,3,1,0,2:T(8,128)(2,1)} %copy.14), calls=%async_computation.1 | async-start | bytes 50331648 | tf_op jit(solution)/shard_map/all_to_all | solution.py:125
  1050.6 14.6 copy-start.4
  1050.6 14.6 copy-start.6
  1056.4 282.6 %all-to-all-start.2 = ((bf16[6,8,128,1024]{3,2,0,1:T(8,128)(2,1)}), bf16[6,8,128,1024]{3,2,0,1:T(8,128)(2,1)}, u32[]{:S(2)}, u32[]{:S(2)}) async-start(bf16[6,8,128,1024]{3,2,0,1:T(8,128)(2,1)} %copy.18), calls=%async_computation.2 | async-start | bytes 25165824 | tf_op jit(solution)/shard_map/all_to_all | solution.py:137
  1065.1 517.8 %all-gather.2.cloned.1.call-start = ((), (), s32[]{:S(2)}) async-start(), calls=%async_computation.3 | async-start | bytes 31457280 | tf_op jit(solution)/shard_map/all_gather | solution.py:140
  1345.3 2.8 copy-start.2
  1353.3 2.7 copy-start
Sparse Core Ops, SparseCore 0:
  1356.2 226.6 all-gather.1

commit v2 on v0

v2 whole, which is shorter than its diff:
```python
import jax
import jax.numpy as jnp
from jax import lax
from jax.experimental import pallas as pl
from jax.experimental.pallas import tpu as pltpu
from jax.sharding import PartitionSpec as P


def split(value):
    high = lax.reduce_precision(value, 8, 7)
    low = value - high
    return high.astype(jnp.bfloat16), low.astype(jnp.bfloat16)


def product(left, right):
    return jnp.dot(left, right, preferred_element_type=jnp.float32)


def call(kernel, table, steps, ins, outs):
    return pl.pallas_call(
        kernel,
        grid_spec=pltpu.PrefetchScalarGridSpec(
            num_scalar_prefetch=1,
            grid=(steps,),
            in_specs=[pl.BlockSpec(shape, index) for _, shape, index in ins],
            out_specs=[pl.BlockSpec((1,) + o.shape[1:], lambda s, t: (s, 0, 0)) for o in outs],
        ),
        out_shape=outs,
        compiler_params=pltpu.CompilerParams(vmem_limit_bytes=32 * 1024 * 1024),
    )(table, *[array for array, _, _ in ins])


def choose(table, stride, sources):
    tile = (1,) + sources[0].shape[-2:]

    def index_of(column):
        def index(s, t):
            return (jnp.where(t[stride * s] == column, t[stride * s + 1], 0), 0, 0)
        return index

    return [(source, tile, index_of(column)) for column, source in enumerate(sources)]


def reorder(table, array):
    tile = (1,) + array.shape[1:]

    def kernel(t, source, out):
        out[...] = source[...]

    out = jax.ShapeDtypeStruct(table.shape + array.shape[1:], array.dtype)
    return call(
        kernel, table, table.shape[0], [(array, tile, lambda s, t: (t[s], 0, 0))], [out]
    )[0]


def pack(table, steps, chunks, moments):
    groups = len(chunks[0])
    _, rows, width = chunks[0][0].shape

    def kernel(t, *refs):
        sources, moment_ref, packed, squares = refs[:-3], refs[-3], refs[-2], refs[-1]
        part = t[3 * pl.program_id(0)]

        @pl.when(part < 0)
        def _():
            packed[...] = jnp.zeros_like(packed)

        for column in range(len(chunks)):

            @pl.when(part == column)
            def _(column=column):
                total = sources[column * groups][0].astype(jnp.float32)
                for replica in range(1, groups):
                    total = total + sources[column * groups + replica][0].astype(jnp.float32)
                packed[0] = total

        total = packed[0]
        moment = 0.95 * moment_ref[0].astype(jnp.float32) + 0.05 * total * total
        adam_step = total / (jnp.sqrt(moment) + 1e-08)
        square = adam_step * adam_step
        squares[0] = jnp.sum(square.reshape(rows // 8, 8, width), axis=0)

    def index_of(column):
        def index(s, t):
            return (jnp.where(t[3 * s] == column, t[3 * s + 1], 0), 0, 0)
        return index

    ins = [(a, (1, rows, width), index_of(i)) for i, c in enumerate(chunks) for a in c]
    ins.append((moments, (1, rows, width), lambda s, t: (t[3 * s + 2], 0, 0)))
    outs = [
        jax.ShapeDtypeStruct((steps, rows, width), jnp.float32),
        jax.ShapeDtypeStruct((steps, 8, width), jnp.float32),
    ]
    return call(kernel, table, steps, ins, outs)


def step(table, steps, returned, weights):
    tile = (1,) + weights.shape[1:]

    def kernel(t, *refs):
        sources, weight, out = refs[:-2], refs[-2], refs[-1]
        part = t[3 * pl.program_id(0)]
        for column, source in enumerate(sources):

            @pl.when(part == column)
            def _(source=source):
                stepped = weight[0].astype(jnp.float32) - 0.5 * source[0].astype(jnp.float32)
                mean = jnp.mean(stepped * stepped, axis=1, keepdims=True)
                out[0] = (stepped * lax.rsqrt(mean + 1e-06)).astype(jnp.bfloat16)

    ins = choose(table, 3, returned)
    ins.append((weights, tile, lambda s, t: (t[3 * s + 2], 0, 0)))
    return call(kernel, table, steps, ins, [jax.ShapeDtypeStruct((steps,) + tile[1:], jnp.bfloat16)])[0]


def collect(table, steps, gathered):
    def kernel(t, *refs):
        sources, out = refs[:-1], refs[-1]
        part = t[2 * pl.program_id(0)]
        for column, source in enumerate(sources):

            @pl.when(part == column)
            def _(source=source):
                out[...] = source[...]

    out = jax.ShapeDtypeStruct((steps,) + gathered[0].shape[1:], gathered[0].dtype)
    return call(kernel, table, steps, choose(table, 2, gathered), [out])[0]


def body(gradients, second_moment, inverse_roots, owners, weights):
    groups = lax.axis_size("groups")
    shards = lax.axis_size("shard")
    group = lax.axis_index("groups")
    blocks = owners.shape[0] // groups
    slots = inverse_roots.shape[2]
    rows, width = gradients.shape[2:]

    grouped = owners.reshape(groups, blocks)
    ids = jnp.arange(blocks, dtype=jnp.int32)
    same = grouped[:, :, None] == grouped[:, None, :]
    rank = jnp.sum(same & (ids[None, :] < ids[:, None])[None], axis=2).astype(jnp.int32)
    key = rank * shards + grouped
    place = jnp.sum(key[:, None, :] < key[:, :, None], axis=2).astype(jnp.int32)
    taken = place[:, None, :] == ids[None, :, None]
    block_at = jnp.sum(jnp.where(taken, ids, 0), axis=2).astype(jnp.int32)

    def mine(array):
        return lax.dynamic_index_in_dim(array, group, 0, keepdims=False)

    my_key, my_place, my_block = mine(key), mine(place), mine(block_at)
    key_at = jnp.sum(jnp.where(mine(taken), my_key, 0), axis=1).astype(jnp.int32)

    chunk_in = min(blocks, shards)
    cuts = [(a, min(a + chunk_in, blocks)) for a in range(0, blocks, chunk_in)]
    first = jnp.arange(groups, dtype=jnp.int32)[:, None] * blocks
    chunks = []
    for low, high in cuts:
        ordered = reorder((first + block_at[:, low:high]).reshape(-1), gradients[0])
        ordered = ordered.reshape(groups, high - low, rows, width)
        received = [lax.dynamic_index_in_dim(ordered, group, 0, keepdims=False)]
        for shift in range(1, groups):
            sent = lax.dynamic_index_in_dim(
                ordered, lax.rem(group + shift, groups), 0, keepdims=False
            )
            pairs = [(g, (g + shift) % groups) for g in range(groups)]
            received.append(lax.ppermute(sent, "groups", pairs))
        chunks.append(received)

    parts = 3 if slots % 3 == 0 and blocks % 3 == 0 else 1
    chunk_out = blocks // parts
    returned, gathered, renormed = [], [], []

    def exchange(array):
        return lax.all_to_all(array, "shard", split_axis=0, concat_axis=0, tiled=True)

    def send(slot, after):
        wanted = my_key[None, :] == (slot * shards + jnp.arange(shards, dtype=jnp.int32))[:, None]
        present = jnp.any(wanted, axis=1)
        at = jnp.sum(jnp.where(wanted, my_place, 0), axis=1).astype(jnp.int32)
        source = jnp.sum(jnp.where(wanted, ids, 0), axis=1).astype(jnp.int32)
        table = jnp.stack(
            [jnp.where(present, at // chunk_in, -1), at % chunk_in, source], axis=1
        ).reshape(-1)
        packed, squares = pack(table, shards, chunks[: slot + 1], second_moment)
        squares = jnp.sum(squares, axis=1, keepdims=True)
        packed, squares, _ = lax.optimization_barrier((packed, squares, after))
        return exchange(packed), exchange(squares)

    def compute(slot, arrived, squares):
        high, low = split(arrived.reshape(shards * rows, width))
        left, right = inverse_roots[0, 0, slot, 0], inverse_roots[0, 0, slot, 1]
        right_product = product(high, right) + product(low, right)
        high, low = split(right_product)
        preconditioned = product(left, high) + product(left, low)
        scale = jnp.sqrt(jnp.sum(squares)) / jnp.sqrt(
            jnp.sum(preconditioned * preconditioned) + 1e-06
        )
        return (scale * preconditioned).astype(jnp.bfloat16).reshape(shards, rows, width)

    arrived, squares = send(0, ())
    for slot in range(slots):
        if slot + 1 < slots:
            after = (arrived, returned[-1:], renormed[-1:])
            following = send(slot + 1, after)
            update = compute(slot, arrived, squares)
            update, arrived = lax.optimization_barrier((update, following[0]))
            squares = following[1]
        else:
            update = compute(slot, arrived, squares)
        returned.append(exchange(update))
        if (slot + 1) * parts % slots == 0:
            start = len(gathered) * chunk_out
            keys = key_at[start : start + chunk_out]
            table = jnp.stack(
                [keys // shards, keys % shards, my_block[start : start + chunk_out]], axis=1
            ).reshape(-1)
            renormed.append(step(table, chunk_out, returned, weights))
            gathered.append(lax.all_gather(renormed[-1], "groups", axis=0, tiled=True))

    inner = jnp.arange(groups, dtype=jnp.int32)[:, None] * chunk_out + place % chunk_out
    table = jnp.stack([place // chunk_out, inner], axis=2).reshape(-1)
    return collect(table, groups * blocks, gathered)


def solution(mesh):
    return jax.shard_map(
        body,
        mesh=mesh,
        in_specs=(
            P("groups", None, "shard", None),
            P("groups", "shard", None),
            P("groups", "shard", None, None, None, None),
            P(),
            P("groups", "shard", None),
        ),
        out_specs=P(None, "shard", None),
        check_vma=False,
    )
```

time: 2200 us -> 1430 us (0.65)
  waiting for transfers between devices: 1480 us -> 866 us
  blocking collectives: 397 us -> 62 us
  Pallas kernels: 0 us -> 172 us
  starting transfers between devices: 15.1 us -> 83.6 us
  local copies, waits for them, and re-layouts: 117 us -> 53.9 us
  other arithmetic: 80.2 us -> 49.9 us
  matrix products: 93 us -> 115 us
    psum x1 -> x0, waiting for transfers between devices: 852 us -> none  [body(): summed = lax.psum(replica_grads, 'groups')]
    psum x1 -> x0, blocking collectives: 397 us -> none  [body(): graft_all = lax.psum(partial_sq, 'shard')]
    all_to_all x2 -> x16, waiting for transfers between devices: 400 us -> 615 us  [exchange(): lax.all_to_all(array, 'shard', split_axis=0, concat_axis=0, tiled=True)]
    pallas_call x0 -> x13, Pallas kernels: none -> 172 us  [call(): pl.pallas_call(kernel, grid_spec=pltpu.PrefetchScalarGridSpec(num_scalar_...]
    ppermute x0 -> x9, waiting for transfers between devices: none -> 164 us  [body(): received.append(lax.ppermute(sent, 'groups', pairs))]
    all_gather x1 -> x3, waiting for transfers between devices: 228 us -> 86.3 us  [body(): gathered.append(lax.all_gather(renormed[-1], 'groups', axis=0, tiled=True))]
    all_to_all x0 -> x2, blocking collectives: none -> 62 us  [exchange(): lax.all_to_all(array, 'shard', split_axis=0, concat_axis=0, tiled=True)]
    all_to_all x2 -> x16, starting transfers between devices: 15 us -> 68.5 us  [exchange(): lax.all_to_all(array, 'shard', split_axis=0, concat_axis=0, tiled=True)]
  transfers between devices with their start and end apart: 4 -> 28, of which waited for: 4 -> 18; matrix products, arithmetic and copies ran while one was open for 1% -> 12% of each run, Pallas kernels for 0% -> 7%
where the time goes in v2:
time: 1430 us; the launch traced here: 1420 us
  waiting for transfers between devices  866 us (61%)
  Pallas kernels  172 us (12%)
  matrix products  115 us (8%)
  starting transfers between devices  83.6 us (6%)
  blocking collectives  62 us (4%)
  local copies, waits for them, and re-layouts  53.9 us (4%)
  other arithmetic  49.9 us (3%)
  between operations  22.4 us (2%)
    all_to_all x16, waiting for transfers between devices, exchange(): lax.all_to_all(array, 'shard', split_axis=0, concat_axis=0, tiled=True)  615 us
    pallas_call x13, Pallas kernels, call(): pl.pallas_call(kernel, grid_spec=pltpu.PrefetchScalarGridSpec(num_scalar_...  172 us
    ppermute x9, waiting for transfers between devices, body(): received.append(lax.ppermute(sent, 'groups', pairs))  164 us
    dot_general x24, matrix products, product(): return jnp.dot(left, right, preferred_element_type=jnp.float32)  115 us
    all_gather x3, waiting for transfers between devices, body(): gathered.append(lax.all_gather(renormed[-1], 'groups', axis=0, tiled=True))  86.3 us
    all_to_all x16, starting transfers between devices, exchange(): lax.all_to_all(array, 'shard', split_axis=0, concat_axis=0, tiled=True)  68.5 us
    all_to_all x2, blocking collectives, exchange(): lax.all_to_all(array, 'shard', split_axis=0, concat_axis=0, tiled=True)  62 us
    unnamed x60, local copies, waits for them, and re-layouts  37.5 us
  transfers between devices with their start and end apart: 28, of which 18 were waited for; matrix products, arithmetic and copies ran while one was open for 12% of the time, Pallas kernels for 7%

profile of v2, /device:TPU:0, one launch (start us, length us, event | category | flops | bytes accessed | tf_op | source)
XLA Modules:
  0.0 1424.6 jit_solution(9501655527392131688)
XLA Ops:
  8.0 16.6 %shard_map.55 = bf16[32,128,1024]{2,1,0:T(8,128)(2,1)S(1)} custom-call(s32[32]{0:T(128)S(1)} %reshape.725.t, bf16[96,128,1024]{2,1,0:T(8,128)(2,1)} %bitcast.335), custom_call_target="tpu_custom_call" | custom-call | tf_op jit(solution)/shard_map/pallas_call | solution.py:20
  36.7 41.6 %collective-permute-done.refs_1_ = bf16[8,128,1024]{2,1,0:T(8,128)(2,1)} collective-permute-done((bf16[8,128,1024]{2,1,0:T(8,128)(2,1)}, bf16[8,128,1024]{2,1,0:T(8,128)(2,1)}, u32[]{:S(2)}, u32[]{:S(2)}) %collective-permute-start) | collective-permute-done | bytes 2097184 | tf_op jit(solution)/shard_map/ppermute | solution.py:166
  78.3 44.1 %collective-permute-done.1.refs_2_ = bf16[8,128,1024]{2,1,0:T(8,128)(2,1)} collective-permute-done((bf16[8,128,1024]{2,1,0:T(8,128)(2,1)}, bf16[8,128,1024]{2,1,0:T(8,128)(2,1)}, u32[]{:S(2)}, u32[]{:S(2)}) %collective-permute-start.1) | collective-permute-done | bytes 2097184 | tf_op jit(solution)/shard_map/ppermute | solution.py:166
  125.4 7.4 shard_map.56
  135.6 4.9 all-to-all-start.1
  140.5 16.6 %shard_map.57 = bf16[32,128,1024]{2,1,0:T(8,128)(2,1)S(1)} custom-call(s32[32]{0:T(128)S(1)} %reshape.729.t, bf16[96,128,1024]{2,1,0:T(8,128)(2,1)} %bitcast.336), custom_call_target="tpu_custom_call" | custom-call | tf_op jit(solution)/shard_map/pallas_call | solution.py:20
  165.1 69.5 %all-to-all-done.1 = f32[8,128,1024]{2,1,0:T(8,128)} async-done(((f32[8,128,1024]{2,1,0:T(8,128)}), f32[8,128,1024]{2,1,0:T(8,128)}, u32[]{:S(2)}, u32[]{:S(2)}) %all-to-all-start.1) | async-done | bytes 4194336 | tf_op jit(solution)/shard_map/all_to_all | solution.py:174
  238.1 16.8 %collective-permute-done.4.refs_6_ = bf16[8,128,1024]{2,1,0:T(8,128)(2,1)} collective-permute-done((bf16[8,128,1024]{2,1,0:T(8,128)(2,1)}, bf16[8,128,1024]{2,1,0:T(8,128)(2,1)}, u32[]{:S(2)}, u32[]{:S(2)}) %collective-permute-start.4) | collective-permute-done | bytes 2097184 | tf_op jit(solution)/shard_map/ppermute | solution.py:166
  256.5 8.2 shard_map.58
  267.4 5.1 all-to-all-start.2
  288.9 6.7 multiply_reduce_fusion.5
  300.4 66.1 %all-to-all-done.2 = f32[8,128,1024]{2,1,0:T(8,128)} async-done(((f32[8,128,1024]{2,1,0:T(8,128)}), f32[8,128,1024]{2,1,0:T(8,128)}, u32[]{:S(2)}, u32[]{:S(2)}) %all-to-all-start.2) | async-done | bytes 4194336 | tf_op jit(solution)/shard_map/all_to_all | solution.py:174
  366.5 4.4 all-to-all-start.3
  371.0 16.6 %shard_map.59 = bf16[32,128,1024]{2,1,0:T(8,128)(2,1)S(1)} custom-call(s32[32]{0:T(128)S(1)} %reshape.733.t, bf16[96,128,1024]{2,1,0:T(8,128)(2,1)} %bitcast.337), custom_call_target="tpu_custom_call" | custom-call | tf_op jit(solution)/shard_map/pallas_call | solution.py:20
  395.2 24.8 %all-to-all-done.3.refs_0_ = bf16[8,128,1024]{2,1,0:T(8,128)(2,1)} async-done(((bf16[8,128,1024]{2,1,0:T(8,128)(2,1)}), bf16[8,128,1024]{2,1,0:T(8,128)(2,1)}, u32[]{:S(2)}, u32[]{:S(2)}) %all-to-all-start.3) | async-done | bytes 2097184 | tf_op jit(solution)/shard_map/all_to_all | solution.py:174
  423.4 17.4 %collective-permute-done.6.refs_9_ = bf16[8,128,1024]{2,1,0:T(8,128)(2,1)} collective-permute-done((bf16[8,128,1024]{2,1,0:T(8,128)(2,1)}, bf16[8,128,1024]{2,1,0:T(8,128)(2,1)}, u32[]{:S(2)}, u32[]{:S(2)}) %collective-permute-start.6) | collective-permute-done | bytes 2097184 | tf_op jit(solution)/shard_map/ppermute | solution.py:166
  440.8 44.3 %collective-permute-done.7.refs_10_ = bf16[8,128,1024]{2,1,0:T(8,128)(2,1)} collective-permute-done((bf16[8,128,1024]{2,1,0:T(8,128)(2,1)}, bf16[8,128,1024]{2,1,0:T(8,128)(2,1)}, u32[]{:S(2)}, u32[]{:S(2)}) %collective-permute-start.7) | collective-permute-done | bytes 2097184 | tf_op jit(solution)/shard_map/ppermute | solution.py:166
  488.4 9.4 shard_map.60
  498.4 5.4 all-to-all-start.5
  520.2 6.7 multiply_reduce_fusion.4
  531.7 66.1 %all-to-all-done.5 = f32[8,128,1024]{2,1,0:T(8,128)} async-done(((f32[8,128,1024]{2,1,0:T(8,128)}), f32[8,128,1024]{2,1,0:T(8,128)}, u32[]{:S(2)}, u32[]{:S(2)}) %all-to-all-start.5) | async-done | bytes 4194336 | tf_op jit(solution)/shard_map/all_to_all | solution.py:174
  597.8 4.4 all-to-all-start.6
  602.2 49.0 %all-to-all-done.6.refs_1_ = bf16[8,128,1024]{2,1,0:T(8,128)(2,1)} async-done(((bf16[8,128,1024]{2,1,0:T(8,128)(2,1)}), bf16[8,128,1024]{2,1,0:T(8,128)(2,1)}, u32[]{:S(2)}, u32[]{:S(2)}) %all-to-all-start.6) | async-done | bytes 2097184 | tf_op jit(solution)/shard_map/all_to_all | solution.py:174
  658.1 8.5 shard_map.62
  670.1 5.6 shard_map.61
  677.1 5.3 all-to-all-start.8
  698.7 6.7 multiply_reduce_fusion.3
  710.3 66.0 %all-to-all-done.8 = f32[8,128,1024]{2,1,0:T(8,128)} async-done(((f32[8,128,1024]{2,1,0:T(8,128)}), f32[8,128,1024]{2,1,0:T(8,128)}, u32[]{:S(2)}, u32[]{:S(2)}) %all-to-all-start.8) | async-done | bytes 4194336 | tf_op jit(solution)/shard_map/all_to_all | solution.py:174
  780.8 49.0 %all-to-all-done.9.refs_2_ = bf16[8,128,1024]{2,1,0:T(8,128)(2,1)} async-done(((bf16[8,128,1024]{2,1,0:T(8,128)(2,1)}), bf16[8,128,1024]{2,1,0:T(8,128)(2,1)}, u32[]{:S(2)}, u32[]{:S(2)}) %all-to-all-start.9) | async-done | bytes 2097184 | tf_op jit(solution)/shard_map/all_to_all | solution.py:174
  836.5 8.0 shard_map.63
  845.2 5.0 all-to-all-start.11
  867.7 6.7 multiply_reduce_fusion.2
  879.2 65.1 %all-to-all-done.11 = f32[8,128,1024]{2,1,0:T(8,128)} async-done(((f32[8,128,1024]{2,1,0:T(8,128)}), f32[8,128,1024]{2,1,0:T(8,128)}, u32[]{:S(2)}, u32[]{:S(2)}) %all-to-all-start.11) | async-done | bytes 4194336 | tf_op jit(solution)/shard_map/all_to_all | solution.py:174
  948.7 49.0 %all-to-all-done.12.refs_3_ = bf16[8,128,1024]{2,1,0:T(8,128)(2,1)} async-done(((bf16[8,128,1024]{2,1,0:T(8,128)(2,1)}), bf16[8,128,1024]{2,1,0:T(8,128)(2,1)}, u32[]{:S(2)}, u32[]{:S(2)}) %all-to-all-start.12) | async-done | bytes 2097184 | tf_op jit(solution)/shard_map/all_to_all | solution.py:174
  1004.7 8.0 shard_map.65
  1015.6 7.2 shard_map.64
  1022.7 10.5 all_to_all.90
  1033.3 4.6 all-to-all-start.14
  1046.7 6.0 fusion.78
  1052.8 5.3 fusion.14
  1058.1 6.5 multiply_reduce_fusion.1
  1070.9 60.9 %all-to-all-done.14 = f32[8,128,1024]{2,1,0:T(8,128)} async-done(((f32[8,128,1024]{2,1,0:T(8,128)}), f32[8,128,1024]{2,1,0:T(8,128)}, u32[]{:S(2)}, u32[]{:S(2)}) %all-to-all-start.14) | async-done | bytes 4194336 | tf_op jit(solution)/shard_map/all_to_all | solution.py:174
  1147.1 6.6 multiply_reduce_fusion
  1157.0 51.5 %all_to_all.91.refs_5_ = bf16[8,128,1024]{2,1,0:T(8,128)(2,1)S(1)} all-to-all(bf16[8,128,1024]{2,1,0:T(8,128)(2,1)S(1)} %bitcast.343), channel_id=1, replica_groups=mesh['groups'=4,'shard'=8] {'shard'}, dimensions={0} | all-to-all | bytes 4194304 | tf_op jit(solution)/shard_map/all_to_all | solution.py:174
  1213.1 48.8 %all-to-all-done.15.refs_4_ = bf16[8,128,1024]{2,1,0:T(8,128)(2,1)} async-done(((bf16[8,128,1024]{2,1,0:T(8,128)(2,1)}), bf16[8,128,1024]{2,1,0:T(8,128)(2,1)}, u32[]{:S(2)}, u32[]{:S(2)}) %all-to-all-start.15) | async-done | bytes 2097184 | tf_op jit(solution)/shard_map/all_to_all | solution.py:174
  1264.7 7.3 shard_map.66
  1272.4 86.3 %all-gather.8.cloned.1.call-done.refs_2_ = bf16[32,128,1024]{2,1,0:T(8,128)(2,1)} async-done(((bf16[8,128,1024]{2,1,0:T(8,128)(2,1)}), bf16[32,128,1024]{2,1,0:T(8,128)(2,1)}) %all-gather.8.cloned.1.call-update) | async-done | bytes 8388624 | tf_op jit(solution)/shard_map/all_gather | solution.py:218
  1365.5 52.4 %shard_map.67 = bf16[96,128,1024]{2,1,0:T(8,128)(2,1)} custom-call(s32[192]{0:T(256)S(1)} %reshape.722.t, bf16[32,128,1024]{2,1,0:T(8,128)(2,1)S(1)} %copy-done.14, bf16[32,128,1024]{2,1,0:T(8,128)(2,1)S(1)} %copy-done.15, bf16[32,128,1024]{2,1,0:T(8,128)(2,1)} %all-gather.8.cloned.1.call-done.refs_2_), custom_call_target="tpu_custom_call" | custom-call | tf_op jit(solution)/shard_map/pallas_call | solution.py:20
  (205 shorter events, 213.4 us)
Async XLA Ops:
  7.7 25.8 %copy-start.18 = (s32[4,24]{1,0:T(4,128)}, s32[4,24]{1,0:T(4,128)S(1)}, u32[]{:S(2)}) copy-start(s32[4,24]{1,0:T(4,128)S(1)} %convert_reduce_fusion) | copy-start | bytes 1156
  27.5 50.7 %collective-permute-start = (bf16[8,128,1024]{2,1,0:T(8,128)(2,1)}, bf16[8,128,1024]{2,1,0:T(8,128)(2,1)}, u32[]{:S(2)}, u32[]{:S(2)}) collective-permute-start(bf16[8,128,1024]{2,1,0:T(8,128)(2,1)} %get-tuple-element.107), channel_id=1, source_target_pairs={{0,8},{8,16},{16,24},{24,0},{1,9},{9,17},{17,25},{25,1},{2,10},{10... | collective-permute-start | bytes 6291464 | tf_op jit(solution)/shard_map/ppermute | solution.py:166
  30.5 91.8 %collective-permute-start.1 = (bf16[8,128,1024]{2,1,0:T(8,128)(2,1)}, bf16[8,128,1024]{2,1,0:T(8,128)(2,1)}, u32[]{:S(2)}, u32[]{:S(2)}) collective-permute-start(bf16[8,128,1024]{2,1,0:T(8,128)(2,1)} %get-tuple-element.106), channel_id=1, source_target_pairs={{0,16},{8,24},{16,0},{24,8},{1,17},{9,25},{17,1},{25,9},{2,18},{10... | collective-permute-start | bytes 6291464 | tf_op jit(solution)/shard_map/ppermute | solution.py:166
  32.0 90.6 %collective-permute-start.2 = (bf16[8,128,1024]{2,1,0:T(8,128)(2,1)}, bf16[8,128,1024]{2,1,0:T(8,128)(2,1)}, u32[]{:S(2)}, u32[]{:S(2)}) collective-permute-start(bf16[8,128,1024]{2,1,0:T(8,128)(2,1)} %get-tuple-element.105), channel_id=1, source_target_pairs={{0,24},{8,0},{16,8},{24,16},{1,25},{9,1},{17,9},{25,17},{2,26},{10... | collective-permute-start | bytes 6291464 | tf_op jit(solution)/shard_map/ppermute | solution.py:166
  122.6 2.8 copy-start
  132.9 2.0 copy-start.17
  135.6 99.0 %all-to-all-start.1 = ((f32[8,128,1024]{2,1,0:T(8,128)}), f32[8,128,1024]{2,1,0:T(8,128)}, u32[]{:S(2)}, u32[]{:S(2)}) async-start(f32[8,128,1024]{2,1,0:T(8,128)} %copy-done.17), calls=%async_computation.1 | async-start | bytes 8388608 | tf_op jit(solution)/shard_map/all_to_all | solution.py:174
  160.7 77.4 %collective-permute-start.3 = (bf16[8,128,1024]{2,1,0:T(8,128)(2,1)}, bf16[8,128,1024]{2,1,0:T(8,128)(2,1)}, u32[]{:S(2)}, u32[]{:S(2)}) collective-permute-start(bf16[8,128,1024]{2,1,0:T(8,128)(2,1)} %get-tuple-element.103), channel_id=1, source_target_pairs={{0,8},{8,16},{16,24},{24,0},{1,9},{9,17},{17,25},{25,1},{2,10},{10... | collective-permute-start | bytes 6291464 | tf_op jit(solution)/shard_map/ppermute | solution.py:166
  162.4 92.5 %collective-permute-start.4 = (bf16[8,128,1024]{2,1,0:T(8,128)(2,1)}, bf16[8,128,1024]{2,1,0:T(8,128)(2,1)}, u32[]{:S(2)}, u32[]{:S(2)}) collective-permute-start(bf16[8,128,1024]{2,1,0:T(8,128)(2,1)} %get-tuple-element.102), channel_id=1, source_target_pairs={{0,16},{8,24},{16,0},{24,8},{1,17},{9,25},{17,1},{25,9},{2,18},{10... | collective-permute-start | bytes 6291464 | tf_op jit(solution)/shard_map/ppermute | solution.py:166
  162.9 92.0 %collective-permute-start.5 = (bf16[8,128,1024]{2,1,0:T(8,128)(2,1)}, bf16[8,128,1024]{2,1,0:T(8,128)(2,1)}, u32[]{:S(2)}, u32[]{:S(2)}) collective-permute-start(bf16[8,128,1024]{2,1,0:T(8,128)(2,1)} %get-tuple-element.101), channel_id=1, source_target_pairs={{0,24},{8,0},{16,8},{24,16},{1,25},{9,1},{17,9},{25,17},{2,26},{10... | collective-permute-start | bytes 6291464 | tf_op jit(solution)/shard_map/ppermute | solution.py:166
  234.6 32.8 %all-to-all-start = ((f32[8,1,1024]{2,1,0:T(1,128)}), f32[8,1,1024]{2,1,0:T(1,128)S(1)}, u32[]{:S(2)}, u32[]{:S(2)}) async-start(f32[8,1,1024]{2,1,0:T(1,128)} %broadcast_in_dim.111), calls=%async_computation | async-start | bytes 65536 | tf_op jit(solution)/shard_map/all_to_all | solution.py:174
  264.7 2.0 copy-start.16
  267.4 99.1 %all-to-all-start.2 = ((f32[8,128,1024]{2,1,0:T(8,128)}), f32[8,128,1024]{2,1,0:T(8,128)}, u32[]{:S(2)}, u32[]{:S(2)}) async-start(f32[8,128,1024]{2,1,0:T(8,128)} %copy-done.16), calls=%async_computation.2 | async-start | bytes 8388608 | tf_op jit(solution)/shard_map/all_to_all | solution.py:174
  366.5 53.4 %all-to-all-start.3 = ((bf16[8,128,1024]{2,1,0:T(8,128)(2,1)}), bf16[8,128,1024]{2,1,0:T(8,128)(2,1)}, u32[]{:S(2)}, u32[]{:S(2)}) async-start(bf16[8,128,1024]{2,1,0:T(8,128)(2,1)} %bitcast.339), calls=%async_computation.3 | async-start | bytes 4194304 | tf_op jit(solution)/shard_map/all_to_all | solution.py:174
  391.1 49.7 %collective-permute-start.6 = (bf16[8,128,1024]{2,1,0:T(8,128)(2,1)}, bf16[8,128,1024]{2,1,0:T(8,128)(2,1)}, u32[]{:S(2)}, u32[]{:S(2)}) collective-permute-start(bf16[8,128,1024]{2,1,0:T(8,128)(2,1)} %get-tuple-element.99), channel_id=1, source_target_pairs={{0,8},{8,16},{16,24},{24,0},{1,9},{9,17},{17,25},{25,1},{2,10},{10... | collective-permute-start | bytes 6291464 | tf_op jit(solution)/shard_map/ppermute | solution.py:166
  392.8 92.3 %collective-permute-start.7 = (bf16[8,128,1024]{2,1,0:T(8,128)(2,1)}, bf16[8,128,1024]{2,1,0:T(8,128)(2,1)}, u32[]{:S(2)}, u32[]{:S(2)}) collective-permute-start(bf16[8,128,1024]{2,1,0:T(8,128)(2,1)} %get-tuple-element.98), channel_id=1, source_target_pairs={{0,16},{8,24},{16,0},{24,8},{1,17},{9,25},{17,1},{25,9},{2,18},{10... | collective-permute-start | bytes 6291464 | tf_op jit(solution)/shard_map/ppermute | solution.py:166
  393.4 91.8 %collective-permute-start.8 = (bf16[8,128,1024]{2,1,0:T(8,128)(2,1)}, bf16[8,128,1024]{2,1,0:T(8,128)(2,1)}, u32[]{:S(2)}, u32[]{:S(2)}) collective-permute-start(bf16[8,128,1024]{2,1,0:T(8,128)(2,1)} %get-tuple-element.97), channel_id=1, source_target_pairs={{0,24},{8,0},{16,8},{24,16},{1,25},{9,1},{17,9},{25,17},{2,26},{10... | collective-permute-start | bytes 6291464 | tf_op jit(solution)/shard_map/ppermute | solution.py:166
  419.9 78.5 %all-to-all-start.4 = ((f32[8,1,1024]{2,1,0:T(1,128)}), f32[8,1,1024]{2,1,0:T(1,128)S(1)}, u32[]{:S(2)}, u32[]{:S(2)}) async-start(f32[8,1,1024]{2,1,0:T(1,128)} %broadcast_in_dim.113), calls=%async_computation.4 | async-start | bytes 65536 | tf_op jit(solution)/shard_map/all_to_all | solution.py:174
  498.4 99.4 %all-to-all-start.5 = ((f32[8,128,1024]{2,1,0:T(8,128)}), f32[8,128,1024]{2,1,0:T(8,128)}, u32[]{:S(2)}, u32[]{:S(2)}) async-start(f32[8,128,1024]{2,1,0:T(8,128)} %get-tuple-element.51), calls=%async_computation.5 | async-start | bytes 8388608 | tf_op jit(solution)/shard_map/all_to_all | solution.py:174
  597.8 53.4 %all-to-all-start.6 = ((bf16[8,128,1024]{2,1,0:T(8,128)(2,1)}), bf16[8,128,1024]{2,1,0:T(8,128)(2,1)}, u32[]{:S(2)}, u32[]{:S(2)}) async-start(bf16[8,128,1024]{2,1,0:T(8,128)(2,1)} %bitcast.340), calls=%async_computation.6 | async-start | bytes 4194304 | tf_op jit(solution)/shard_map/all_to_all | solution.py:174
  651.3 25.8 %all-to-all-start.7 = ((f32[8,1,1024]{2,1,0:T(1,128)}), f32[8,1,1024]{2,1,0:T(1,128)S(1)}, u32[]{:S(2)}, u32[]{:S(2)}) async-start(f32[8,1,1024]{2,1,0:T(1,128)} %broadcast_in_dim.115), calls=%async_computation.7 | async-start | bytes 65536 | tf_op jit(solution)/shard_map/all_to_all | solution.py:174
  667.4 2.8 copy-start.6
  677.1 99.3 %all-to-all-start.8 = ((f32[8,128,1024]{2,1,0:T(8,128)}), f32[8,128,1024]{2,1,0:T(8,128)}, u32[]{:S(2)}, u32[]{:S(2)}) async-start(f32[8,128,1024]{2,1,0:T(8,128)} %get-tuple-element.57), calls=%async_computation.8 | async-start | bytes 8388608 | tf_op jit(solution)/shard_map/all_to_all | solution.py:174
  706.1 74.6 %copy-start.28 = (s32[8]{0:T(128)S(1)}, s32[8]{0:T(128)}, u32[]{:S(2)}) copy-start(s32[8]{0:T(128)} %get-tuple-element.92) | copy-start | bytes 100
  706.2 74.6 %copy-start.26 = (pred[8]{0:T(512)(128)(4,1)S(1)}, pred[8]{0:T(512)(128)(4,1)}, u32[]{:S(2)}) copy-start(pred[8]{0:T(512)(128)(4,1)} %get-tuple-element.88) | copy-start | bytes 28
  706.2 74.6 %copy-start.27 = (s32[8]{0:T(128)S(1)}, s32[8]{0:T(128)}, u32[]{:S(2)}) copy-start(s32[8]{0:T(128)} %get-tuple-element.81) | copy-start | bytes 100
  706.2 127.0 %copy-start.20 = (s32[8]{0:T(128)S(1)}, s32[8]{0:T(128)}, u32[]{:S(2)}) copy-start(s32[8]{0:T(128)} %get-tuple-element.82) | copy-start | bytes 100
  706.2 127.0 %copy-start.21 = (s32[8,1]{0,1:T(1,128)S(1)}, s32[8,1]{0,1:T(1,128)}, u32[]{:S(2)}) copy-start(s32[8,1]{0,1:T(1,128)} %get-tuple-element.91) | copy-start | bytes 100
  706.2 127.0 %copy-start.22 = (s32[8,1]{0,1:T(1,128)S(1)}, s32[8,1]{0,1:T(1,128)}, u32[]{:S(2)}) copy-start(s32[8,1]{0,1:T(1,128)} %get-tuple-element.132) | copy-start | bytes 100
  776.4 53.4 %all-to-all-start.9 = ((bf16[8,128,1024]{2,1,0:T(8,128)(2,1)}), bf16[8,128,1024]{2,1,0:T(8,128)(2,1)}, u32[]{:S(2)}, u32[]{:S(2)}) async-start(bf16[8,128,1024]{2,1,0:T(8,128)(2,1)} %bitcast.341), calls=%async_computation.9 | async-start | bytes 4194304 | tf_op jit(solution)/shard_map/all_to_all | solution.py:174
  829.8 15.5 %all-to-all-start.10 = ((f32[8,1,1024]{2,1,0:T(1,128)}), f32[8,1,1024]{2,1,0:T(1,128)S(1)}, u32[]{:S(2)}, u32[]{:S(2)}) async-start(f32[8,1,1024]{2,1,0:T(1,128)} %broadcast_in_dim.117), calls=%async_computation.10 | async-start | bytes 65536 | tf_op jit(solution)/shard_map/all_to_all | solution.py:174
  845.2 99.1 %all-to-all-start.11 = ((f32[8,128,1024]{2,1,0:T(8,128)}), f32[8,128,1024]{2,1,0:T(8,128)}, u32[]{:S(2)}, u32[]{:S(2)}) async-start(f32[8,128,1024]{2,1,0:T(8,128)} %get-tuple-element.63), calls=%async_computation.11 | async-start | bytes 8388608 | tf_op jit(solution)/shard_map/all_to_all | solution.py:174
  850.3 422.1 %all-gather.4.cloned.1.call-start = ((), (), s32[]{:S(2)}) async-start(), calls=%async_computation.18 | async-start | bytes 10485760 | tf_op jit(solution)/shard_map/all_gather | solution.py:218
  875.1 73.6 %copy-start.24 = (pred[8]{0:T(512)(128)(4,1)S(1)}, pred[8]{0:T(512)(128)(4,1)}, u32[]{:S(2)}) copy-start(pred[8]{0:T(512)(128)(4,1)} %get-tuple-element.84) | copy-start | bytes 28
  875.1 73.6 %copy-start.25 = (s32[8]{0:T(128)S(1)}, s32[8]{0:T(128)}, u32[]{:S(2)}) copy-start(s32[8]{0:T(128)} %get-tuple-element.73) | copy-start | bytes 100
  875.1 126.0 %copy-start.23 = (s32[8]{0:T(128)S(1)}, s32[8]{0:T(128)}, u32[]{:S(2)}) copy-start(s32[8]{0:T(128)} %get-tuple-element.74) | copy-start | bytes 100
  944.4 53.4 %all-to-all-start.12 = ((bf16[8,128,1024]{2,1,0:T(8,128)(2,1)}), bf16[8,128,1024]{2,1,0:T(8,128)(2,1)}, u32[]{:S(2)}, u32[]{:S(2)}) async-start(bf16[8,128,1024]{2,1,0:T(8,128)(2,1)} %bitcast.342), calls=%async_computation.12 | async-start | bytes 4194304 | tf_op jit(solution)/shard_map/all_to_all | solution.py:174
  997.8 25.0 %all-to-all-start.13 = ((f32[8,1,1024]{2,1,0:T(1,128)}), f32[8,1,1024]{2,1,0:T(1,128)S(1)}, u32[]{:S(2)}, u32[]{:S(2)}) async-start(f32[8,1,1024]{2,1,0:T(1,128)} %broadcast_in_dim.119), calls=%async_computation.13 | async-start | bytes 65536 | tf_op jit(solution)/shard_map/all_to_all | solution.py:174
  1012.8 2.8 copy-start.7
  1033.3 98.6 %all-to-all-start.14 = ((f32[8,128,1024]{2,1,0:T(8,128)}), f32[8,128,1024]{2,1,0:T(8,128)}, u32[]{:S(2)}, u32[]{:S(2)}) async-start(f32[8,128,1024]{2,1,0:T(8,128)} %get-tuple-element.69), calls=%async_computation.14 | async-start | bytes 8388608 | tf_op jit(solution)/shard_map/all_to_all | solution.py:174
  1037.8 234.6 %all-gather.6.cloned.1.call-start = ((), (), s32[]{:S(2)}) async-start(), calls=%async_computation.19 | async-start | bytes 10485760 | tf_op jit(solution)/shard_map/all_gather | solution.py:218
  1052.8 5.3 copy-start.29
  1208.5 53.4 %all-to-all-start.15 = ((bf16[8,128,1024]{2,1,0:T(8,128)(2,1)}), bf16[8,128,1024]{2,1,0:T(8,128)(2,1)}, u32[]{:S(2)}, u32[]{:S(2)}) async-start(bf16[8,128,1024]{2,1,0:T(8,128)(2,1)} %bitcast.338), calls=%async_computation.15 | async-start | bytes 4194304 | tf_op jit(solution)/shard_map/all_to_all | solution.py:174
  1212.9 145.8 %all-gather.8.cloned.1.call-start = ((), (), s32[]{:S(2)}) async-start(), calls=%async_computation.20 | async-start | bytes 10485760 | tf_op jit(solution)/shard_map/all_gather | solution.py:218
  1262.0 2.8 copy-start.8
  1264.7 7.3 copy-start.19
  1358.7 3.4 copy-start.14
  1362.1 3.4 copy-start.15
  (10 other events, 15.6 us)
Sparse Core Ops, SparseCore 0:
  852.9 89.1 all-gather.3
  1052.9 88.9 all-gather.5
  1272.2 86.5 all-gather.7
